TPU v7x, 32 devices: a whole 2x2x4 slice. The times are simulated.
32 devices in a mesh: query: 2 (over x), gallery: 16 (over z, y, core).
Axes of the slice: x: 2, y: 2, z: 4, core: 2. Of those that a mesh axis runs over, the one named last changes fastest.
Arguments:
- query_hidden: bfloat16 [768, 32, 768], P(('query', 'gallery')), may hold values from -6 to 6
- query_mask: int32 [768, 32], P(('query', 'gallery')), may hold values 0 or 1
- passage_hidden: bfloat16 [16, 360, 768], P('gallery', 'query'), may hold values from -6 to 6
- passage_ids: int32 [16, 360], P('gallery', 'query'), may hold values from 999 to 30521, as said below
- passage_lengths: int32 [32], P('gallery'), may hold values from 30 to 180, as said below
- projection: bfloat16 [768, 128], replicated, may hold values from -0.21875 to 0.21875
Outputs:
- scores: float32 [768, 32], P(('query', 'gallery'))
Inputs may be any that keep to these rules, and one draw needn't show every extreme that they name: `passage_ids`: ids from 999 to 1066 are punctuation; the rest are words. `passage_lengths`: some passage has exactly 180 tokens.
All inputs are finite; a program needn't handle non-finite values. No bound on the sum of `query_mask` on one device may be relied on, other than what follows from the above.
Results may differ from a plain program's by a relative error of at most 0.00036.
Values may be sent and summed in bfloat16 or wider, within the bound.
A program may use at most 64 MiB of HBM per device.

v0:
```python
import math
import jax
import jax.numpy as jnp
from jax import lax
from jax.sharding import PartitionSpec as P

DIM = 128
PLEN = 180
QLEN = 32
PUNCT_LO = 999
PUNCT_HI = 1067
PASS_GRP = 2
EPS = 1e-06
NEG = -1000000000.0


def unit_rows(hidden, projection):
    flat_rows = hidden.reshape(-1, hidden.shape[-1])
    projected = jnp.dot(flat_rows, projection, preferred_element_type=jnp.float32)
    inverse_norm = lax.rsqrt(jnp.sum(projected * projected, axis=-1, keepdims=True) + EPS)
    return (projected * inverse_norm).astype(jnp.bfloat16)


def local(query_hidden, query_mask, passage_hidden, passage_ids, passage_lengths, projection):
    row_count = passage_hidden.shape[1]
    query_count = query_hidden.shape[0]
    groups = lax.axis_size("gallery")
    query_block = lax.axis_index("query")
    position = query_block * row_count + jnp.arange(row_count, dtype=jnp.int32)
    passage_slot = position // PLEN
    token_pos = position % PLEN
    onehot = passage_slot[:, None] == jnp.arange(PASS_GRP, dtype=jnp.int32)[None, :]
    length_rows = jnp.sum(jnp.where(onehot, passage_lengths[None, :], 0), axis=1)
    token_ids = passage_ids[0]
    punctuation = (token_ids >= PUNCT_LO) & (token_ids < PUNCT_HI)
    kept = (token_pos < length_rows) & ((token_pos == 0) | jnp.logical_not(punctuation))
    kept_flag = kept.astype(jnp.bfloat16)[None, :]
    passage_unit = unit_rows(passage_hidden, projection).reshape(1, row_count, DIM)
    query_unit = unit_rows(query_hidden, projection)
    weights = query_mask.astype(jnp.float32).reshape(-1)
    thin_units, thin_flags = (
        lax.all_gather(passage_unit, "gallery", axis=0, tiled=True),
        lax.all_gather(kept_flag, "gallery", axis=0, tiled=True),
    )
    initial = jnp.full((query_unit.shape[0], groups * PASS_GRP), NEG, jnp.float32)
    piece_units = lax.all_gather(thin_units, "query", axis=1, tiled=True)
    piece_flags = lax.all_gather(thin_flags, "query", axis=1, tiled=True)
    piece_rows = piece_units.shape[1]
    row_slot = jnp.arange(piece_rows, dtype=jnp.int32) // PLEN
    block_width = math.gcd(groups, 4)
    unit_blocks = piece_units.reshape(groups // block_width, block_width * piece_rows, DIM)
    flag_blocks = piece_flags.reshape(groups // block_width, 1, block_width * piece_rows)

    def one_block(block_pair):
        unit_block, flag_block = block_pair
        similar = jnp.einsum(
            "td,rd->tr", query_unit, unit_block, preferred_element_type=jnp.float32
        )
        similar = jnp.where(flag_block > 0, similar, NEG).reshape(-1, block_width, piece_rows)
        per_member = [
            jnp.max(jnp.where(row_slot == member, similar, NEG), axis=2)
            for member in range(PASS_GRP)
        ]
        return jnp.stack(per_member, axis=2)

    fresh_max = lax.map(one_block, (unit_blocks, flag_blocks))
    fresh_max = jnp.transpose(fresh_max, (1, 0, 2, 3)).reshape(initial.shape)
    running = jnp.maximum(initial, fresh_max)
    scores = jnp.sum(
        (running * weights[:, None]).reshape(query_count, QLEN, groups * PASS_GRP), axis=1
    )
    return scores


def solution(mesh):
    placed = (
        P(("query", "gallery"), None, None),
        P(("query", "gallery"), None),
        P("gallery", "query", None),
        P("gallery", "query"),
        P("gallery"),
        P(),
    )
    return jax.shard_map(
        local, mesh=mesh, in_specs=placed, out_specs=P(("query", "gallery"), None), check_vma=False
    )
```

profile of v0, /device:TPU:0, one launch (start us, length us, event | category | flops | bytes accessed | tf_op | source)
XLA Modules:
  0.0 77.6 jit_solution(7608371529911874838)
XLA Ops:
  6.5 0.0 copy-start
  6.5 0.0 all-gather.6.cloned.1.call-start
  6.5 1.4 %multiply_reduce_fusion.2 = (f32[180]{0:T(256)S(1)}, f32[180,128]{1,0:T(8,128)S(1)}) fusion(bf16[768,128]{1,0:T(8,128)(2,1)} %param.13, bf16[1,180,768]{2,1,0:T(8,128)(2,1)} %param.10), kind=kOutput, calls=%fused_computation.26 | convolution fusion | flops 35435340 | bytes 565968 | tf_op jit(solution)/shard_map/dot_general | solution.py:19
  8.0 0.1 fusion.11
  8.1 0.0 copy-start.1
  8.1 25.5 %all-gather.3 = bf16[16,180,128]{2,1,0:T(8,128)(2,1)S(1)} all-gather(bf16[1,180,128]{2,1,0:T(8,128)(2,1)S(1)} %fusion.11), channel_id=2, replica_groups=mesh['query'=2,'gallery'=16] {'gallery'}, dimensions={0}, use_global_device_ids=true | all-gather | bytes 783360 | tf_op jit(solution)/shard_map/all_gather | solution.py:42
  33.6 1.0 %copy.25 = bf16[16,180,128]{2,0,1:T(8,128)(2,1)} copy(bf16[16,180,128]{2,1,0:T(8,128)(2,1)S(1)} %all-gather.3) | data formatting | bytes 1474560 | tf_op jit(solution)/shard_map/all_gather | solution.py:42
  34.6 0.0 all-gather.6.cloned.1.call-update
  34.6 0.0 copy-start.4
  34.6 0.0 copy-start.3
  34.7 0.0 copy-done
  34.7 0.0 copy-done.1
  34.7 0.0 copy-start.2
  34.7 0.6 multiply_reduce_fusion.1
  35.3 0.2 copy.28
  35.5 0.0 copy-done.4
  35.5 0.1 fusion.12
  35.6 0.0 copy-done.3
  35.6 17.5 %all-gather.1 = bf16[16,1,180]{2,1,0:T(2,128)(2,1)S(1)} all-gather(bf16[1,1,180]{2,1,0:T(2,128)(2,1)S(1)} %fusion.13), channel_id=1, replica_groups=mesh['query'=2,'gallery'=16] {'gallery'}, dimensions={0}, use_global_device_ids=true | all-gather | bytes 6120 | tf_op jit(solution)/shard_map/all_gather | solution.py:43
  53.1 4.5 %all-gather.2 = bf16[2,180,16]{1,2,0:T(8,128)(2,1)S(1)} all-gather(bf16[1,180,16]{1,2,0:T(8,128)(2,1)S(1)} %bitcast.56), channel_id=1, replica_groups=mesh['query'=2,'gallery'=16] {'query'}, dimensions={0}, use_global_device_ids=true | all-gather | bytes 17280 | tf_op jit(solution)/shard_map/all_gather | solution.py:47
  57.6 0.1 reshape.108
  57.7 0.1 reshape.113
  57.8 0.0 copy-done.2
  57.8 0.5 all-gather.6.cloned.1.call-done
  58.3 1.8 %copy.26 = bf16[16,360,128]{2,1,0:T(8,128)(2,1)S(1)} copy(bf16[16,360,128]{2,0,1:T(8,128)(2,1)} %all-gather.6.cloned.1.call-done) | data formatting | bytes 2949120 | tf_op jit(solution)/shard_map/all_gather | solution.py:46
  60.1 9.6 %while.12 = (s32[]{:T(128)}, f32[4,768,4,2]{1,3,2,0:T(2,128)S(1)}, bf16[4,1,1440]{2,1,0:T(2,128)(2,1)S(1)}, bf16[4,1440,128]{2,1,0:T(8,128)(2,1)S(1)}, bf16[768,128]{1,0:T(8,128)(2,1)S(1)}, /*index=5*/s32[]{:T(128)}) while((s32[]{:T(128)}, f32[4,768,4,2]{1,3,2,0:T(2,128)S(1)}, bf16[4,1,1440]{2,1,0:T(2,128)(2,1)S(1)}, ...), condition=%wide.region_6.7_spmd.clone.clone, body=%wide.region_3.6_spmd.clone.clone.sunk | while | flops 288650176 | bytes 9543377 | solution.py:66
  60.2 1.1 %convolution_select_fusion.2 = f32[1440,768]{1,0:T(8,128)S(1)} fusion(bf16[768,128]{1,0:T(8,128)(2,1)S(1)} %get-tuple-element.172, pred[1440]{0:T(1024)(128)(4,1)S(1)} %compare_reduce_fusion.2, bf16[4,1440,128]{2,1,0:T(8,128)(2,1)S(1)} %get-tuple-element.171, s32[]{:T(128)} %get-tuple-element.162), kind=kOutput, calls=%fused_computation.3.clone.1 | convolution fusion | flops 284221440 | bytes 4990980 | tf_op jit(solution)/shard_map/while/body/eval_jaxpr/td,rd->tr/dot_general | solution.py:56
  61.3 1.1 %select_reduce_fusion.3 = (f32[768,4]{0,1:T(4,128)S(1)}, f32[768,4]{0,1:T(4,128)S(1)}) fusion(f32[768,4,360]{0,2,1:T(8,128)S(1)} %bitcast.53, pred[360]{0:T(512)(128)(4,1)S(1)} %get-tuple-element.152, pred[360]{0:T(512)(128)(4,1)S(1)} %get-tuple-element.153), kind=kLoop, calls=%fused_computation.2.clone.1 | loop fusion | flops 4417536 | bytes 4448976 | tf_op jit(solution)/shard_map/while/body/eval_jaxpr/reduce_max | solution.py:61
  62.5 1.1 %convolution_select_fusion.2 = f32[1440,768]{1,0:T(8,128)S(1)} fusion(bf16[768,128]{1,0:T(8,128)(2,1)S(1)} %get-tuple-element.172, pred[1440]{0:T(1024)(128)(4,1)S(1)} %compare_reduce_fusion.2, bf16[4,1440,128]{2,1,0:T(8,128)(2,1)S(1)} %get-tuple-element.171, s32[]{:T(128)} %get-tuple-element.162), kind=kOutput, calls=%fused_computation.3.clone.1 | convolution fusion | flops 284221440 | bytes 4990980 | tf_op jit(solution)/shard_map/while/body/eval_jaxpr/td,rd->tr/dot_general | solution.py:56
  63.7 1.1 %select_reduce_fusion.3 = (f32[768,4]{0,1:T(4,128)S(1)}, f32[768,4]{0,1:T(4,128)S(1)}) fusion(f32[768,4,360]{0,2,1:T(8,128)S(1)} %bitcast.53, pred[360]{0:T(512)(128)(4,1)S(1)} %get-tuple-element.152, pred[360]{0:T(512)(128)(4,1)S(1)} %get-tuple-element.153), kind=kLoop, calls=%fused_computation.2.clone.1 | loop fusion | flops 4417536 | bytes 4448976 | tf_op jit(solution)/shard_map/while/body/eval_jaxpr/reduce_max | solution.py:61
  64.9 1.1 %convolution_select_fusion.2 = f32[1440,768]{1,0:T(8,128)S(1)} fusion(bf16[768,128]{1,0:T(8,128)(2,1)S(1)} %get-tuple-element.172, pred[1440]{0:T(1024)(128)(4,1)S(1)} %compare_reduce_fusion.2, bf16[4,1440,128]{2,1,0:T(8,128)(2,1)S(1)} %get-tuple-element.171, s32[]{:T(128)} %get-tuple-element.162), kind=kOutput, calls=%fused_computation.3.clone.1 | convolution fusion | flops 284221440 | bytes 4990980 | tf_op jit(solution)/shard_map/while/body/eval_jaxpr/td,rd->tr/dot_general | solution.py:56
  66.1 1.1 %select_reduce_fusion.3 = (f32[768,4]{0,1:T(4,128)S(1)}, f32[768,4]{0,1:T(4,128)S(1)}) fusion(f32[768,4,360]{0,2,1:T(8,128)S(1)} %bitcast.53, pred[360]{0:T(512)(128)(4,1)S(1)} %get-tuple-element.152, pred[360]{0:T(512)(128)(4,1)S(1)} %get-tuple-element.153), kind=kLoop, calls=%fused_computation.2.clone.1 | loop fusion | flops 4417536 | bytes 4448976 | tf_op jit(solution)/shard_map/while/body/eval_jaxpr/reduce_max | solution.py:61
  67.3 1.1 %convolution_select_fusion.2 = f32[1440,768]{1,0:T(8,128)S(1)} fusion(bf16[768,128]{1,0:T(8,128)(2,1)S(1)} %get-tuple-element.172, pred[1440]{0:T(1024)(128)(4,1)S(1)} %compare_reduce_fusion.2, bf16[4,1440,128]{2,1,0:T(8,128)(2,1)S(1)} %get-tuple-element.171, s32[]{:T(128)} %get-tuple-element.162), kind=kOutput, calls=%fused_computation.3.clone.1 | convolution fusion | flops 284221440 | bytes 4990980 | tf_op jit(solution)/shard_map/while/body/eval_jaxpr/td,rd->tr/dot_general | solution.py:56
  68.5 1.1 %select_reduce_fusion.3 = (f32[768,4]{0,1:T(4,128)S(1)}, f32[768,4]{0,1:T(4,128)S(1)}) fusion(f32[768,4,360]{0,2,1:T(8,128)S(1)} %bitcast.53, pred[360]{0:T(512)(128)(4,1)S(1)} %get-tuple-element.152, pred[360]{0:T(512)(128)(4,1)S(1)} %get-tuple-element.153), kind=kLoop, calls=%fused_computation.2.clone.1 | loop fusion | flops 4417536 | bytes 4448976 | tf_op jit(solution)/shard_map/while/body/eval_jaxpr/reduce_max | solution.py:61
  69.7 0.1 maximum_bitcast_fusion.1
  69.7 0.2 max_broadcast_in_dim.12
  69.9 0.2 multiply_reduce_fusion
  70.1 0.7 copy.29
  (29 shorter events, 0.6 us)
Async XLA Ops:
  6.5 28.1 %copy-start = (bf16[24,32,768]{2,1,0:T(8,128)(2,1)S(1)}, bf16[24,32,768]{2,1,0:T(8,128)(2,1)}, u32[]{:S(2)}) copy-start(bf16[24,32,768]{2,1,0:T(8,128)(2,1)} %param.8) | copy-start | bytes 3538948
  6.5 51.8 %all-gather.6.cloned.1.call-start = ((), (), s32[]{:S(2)}) async-start(), calls=%async_computation | async-start | bytes 2211840 | tf_op jit(solution)/shard_map/all_gather | solution.py:46
  8.1 26.6 %copy-start.1 = (bf16[768,128]{1,0:T(8,128)(2,1)S(1)}, bf16[768,128]{1,0:T(8,128)(2,1)}, u32[]{:S(2)}) copy-start(bf16[768,128]{1,0:T(8,128)(2,1)} %param.13) | copy-start | bytes 589828
  34.6 0.9 %copy-start.4 = (s32[2]{0:T(128)S(1)}, s32[2]{0:T(128)}, u32[]{:S(2)}) copy-start(s32[2]{0:T(128)} %param.12) | copy-start | bytes 28
  34.6 1.0 %copy-start.3 = (s32[1,180]{1,0:T(1,128)S(1)}, s32[1,180]{1,0:T(1,128)}, u32[]{:S(2)}) copy-start(s32[1,180]{1,0:T(1,128)} %param.11) | copy-start | bytes 2164
  34.7 23.1 %copy-start.2 = (s32[24,32]{1,0:T(8,128)S(1)}, s32[24,32]{1,0:T(8,128)}, u32[]{:S(2)}) copy-start(s32[24,32]{1,0:T(8,128)} %param.9) | copy-start | bytes 9220
Sparse Core Ops, SparseCore 0:
  34.7 23.5 all-gather.5
where the time goes:
time: 77.8 us; the launch traced here: 77.6 us
  blocking collectives  47.5 us (61%)
  between operations  13.6 us (17%)
  matrix products  6.51 us (8%)
  other arithmetic  5.26 us (7%)
  local copies, waits for them, and re-layouts  4.07 us (5%)
    all_gather x1, blocking collectives, local(): lax.all_gather(passage_unit, 'gallery', axis=0, tiled=True)  25.5 us
    all_gather x1, blocking collectives, local(): lax.all_gather(kept_flag, 'gallery', axis=0, tiled=True)  17.5 us
    dot_general x4, matrix products, one_block(): jnp.einsum('td,rd->tr', query_unit, unit_block, preferred_element_type=jn...  4.52 us
    all_gather x1, blocking collectives, local(): piece_flags = lax.all_gather(thin_flags, 'query', axis=1, tiled=True)  4.49 us
    reduce_max x4, other arithmetic, one_block(): jnp.max(jnp.where(row_slot == member, similar, NEG), axis=2)  4.39 us
    dot_general x2, matrix products, unit_rows(): jnp.dot(flat_rows, projection, preferred_element_type=jnp.float32)  2 us
    all_gather x1, local copies, waits for them, and re-layouts, local(): piece_units = lax.all_gather(thin_units, 'query', axis=1, tiled=True)  1.75 us
  transfers between devices with their start and end apart: 1, of which 1 were waited for; matrix products, arithmetic and copies ran while one was open for 1% of the time, Pallas kernels for 0%

commit v1 on v0

--- a/solution.py
+++ b/solution.py
@@ -12,6 +12,19 @@
 PASS_GRP = 2
 EPS = 1e-06
 NEG = -1000000000.0
+
+
+def gather_around(array, axis, dim):
+    size, index, rows = (lax.axis_size(axis), lax.axis_index(axis), array.shape[dim])
+    ahead = [(i, (i + 1) % size) for i in range(size)]
+    result = jnp.zeros((*array.shape[:dim], size * rows, *array.shape[dim + 1 :]), array.dtype)
+    held = array
+    for step in range(size):
+        source = (index - step) % size
+        result = lax.dynamic_update_slice_in_dim(result, held, source * rows, axis=dim)
+        if step < size - 1:
+            held = lax.ppermute(held, axis, ahead)
+    return result
 
 
 def unit_rows(hidden, projection):
@@ -39,7 +52,7 @@
     query_unit = unit_rows(query_hidden, projection)
     weights = query_mask.astype(jnp.float32).reshape(-1)
     thin_units, thin_flags = (
-        lax.all_gather(passage_unit, "gallery", axis=0, tiled=True),
+        gather_around(passage_unit, "gallery", 0),
         lax.all_gather(kept_flag, "gallery", axis=0, tiled=True),
     )
     initial = jnp.full((query_unit.shape[0], groups * PASS_GRP), NEG, jnp.float32)

time: 77.8 us -> 195 us (2.51)
  waiting for transfers between devices: 0.54 us -> 91.3 us
  local copies, waits for them, and re-layouts: 4.07 us -> 54 us
  blocking collectives: 47.5 us -> 22.7 us
    ppermute x0 -> x15, waiting for transfers between devices: none -> 87.2 us  [gather_around(): held = lax.ppermute(held, axis, ahead)]
    dynamic_update_slice x0 -> x16, local copies, waits for them, and re-layouts: none -> 48.8 us  [gather_around(): lax.dynamic_update_slice_in_dim(result, held, source * rows, axis=dim)]
    all_gather x1 -> x0, blocking collectives: 25.5 us -> none  [local(): lax.all_gather(passage_unit, 'gallery', axis=0, tiled=True)]
    all_gather x1, waiting for transfers between devices: 0.52 us -> 4.11 us  [local(): piece_units = lax.all_gather(thin_units, 'query', axis=1, tiled=True)]
  transfers between devices with their start and end apart: 1 -> 16, of which waited for: 1 -> 15; matrix products, arithmetic and copies ran while one was open for 1% -> 25% of each run, Pallas kernels for 0% -> 0%
where the time goes in v1:
time: 195 us
  waiting for transfers between devices  91.3 us (47%)
  local copies, waits for them, and re-layouts  54 us (28%)
  blocking collectives  22.7 us (12%)
  between operations  14.2 us (7%)
  matrix products  6.51 us (3%)
  other arithmetic  5.26 us (3%)
    ppermute x15, waiting for transfers between devices, gather_around(): held = lax.ppermute(held, axis, ahead)  87.2 us
    dynamic_update_slice x16, local copies, waits for them, and re-layouts, gather_around(): lax.dynamic_update_slice_in_dim(result, held, source * rows, axis=dim)  48.8 us
    all_gather x1, blocking collectives, local(): lax.all_gather(kept_flag, 'gallery', axis=0, tiled=True)  18 us
    all_gather x1, blocking collectives, local(): piece_flags = lax.all_gather(thin_flags, 'query', axis=1, tiled=True)  4.72 us
    dot_general x4, matrix products, one_block(): jnp.einsum('td,rd->tr', query_unit, unit_block, preferred_element_type=jn...  4.51 us
    reduce_max x4, other arithmetic, one_block(): jnp.max(jnp.where(row_slot == member, similar, NEG), axis=2)  4.39 us
    all_gather x1, waiting for transfers between devices, local(): piece_units = lax.all_gather(thin_units, 'query', axis=1, tiled=True)  4.11 us
  transfers between devices with their start and end apart: 16, of which 15 were waited for; matrix products, arithmetic and copies ran while one was open for 25% of the time, Pallas kernels for 0%

profile of v1, /device:TPU:0, one launch (start us, length us, event | category | flops | bytes accessed | tf_op | source)
XLA Modules:
  0.0 194.8 jit_solution(2191806040769500124)
XLA Ops:
  6.5 1.4 multiply_reduce_fusion.2
  8.1 0.5 collective-permute-start
  8.6 6.7 %collective-permute-done = bf16[1,180,128]{2,1,0:T(8,128)(2,1)S(1)} collective-permute-done((bf16[1,180,128]{2,1,0:T(8,128)(2,1)S(1)}, bf16[1,180,128]{2,1,0:T(8,128)(2,1)S(1)}, u32[]{:S(2)}, u32[]{:S(2)}) %collective-permute-start) | collective-permute-done | bytes 46112 | tf_op jit(solution)/shard_map/ppermute | solution.py:26
  15.3 6.2 %collective-permute-done.1 = bf16[1,180,128]{2,1,0:T(8,128)(2,1)S(1)} collective-permute-done((bf16[1,180,128]{2,1,0:T(8,128)(2,1)S(1)}, bf16[1,180,128]{2,1,0:T(8,128)(2,1)S(1)}, u32[]{:S(2)}, u32[]{:S(2)}) %collective-permute-start.1) | collective-permute-done | bytes 46112 | tf_op jit(solution)/shard_map/ppermute | solution.py:26
  21.5 6.2 %collective-permute-done.2 = bf16[1,180,128]{2,1,0:T(8,128)(2,1)S(1)} collective-permute-done((bf16[1,180,128]{2,1,0:T(8,128)(2,1)S(1)}, bf16[1,180,128]{2,1,0:T(8,128)(2,1)S(1)}, u32[]{:S(2)}, u32[]{:S(2)}) %collective-permute-start.2) | collective-permute-done | bytes 46112 | tf_op jit(solution)/shard_map/ppermute | solution.py:26
  27.7 6.2 %collective-permute-done.3 = bf16[1,180,128]{2,1,0:T(8,128)(2,1)S(1)} collective-permute-done((bf16[1,180,128]{2,1,0:T(8,128)(2,1)S(1)}, bf16[1,180,128]{2,1,0:T(8,128)(2,1)S(1)}, u32[]{:S(2)}, u32[]{:S(2)}) %collective-permute-start.3) | collective-permute-done | bytes 46112 | tf_op jit(solution)/shard_map/ppermute | solution.py:26
  33.9 6.2 %collective-permute-done.4 = bf16[1,180,128]{2,1,0:T(8,128)(2,1)S(1)} collective-permute-done((bf16[1,180,128]{2,1,0:T(8,128)(2,1)S(1)}, bf16[1,180,128]{2,1,0:T(8,128)(2,1)S(1)}, u32[]{:S(2)}, u32[]{:S(2)}) %collective-permute-start.4) | collective-permute-done | bytes 46112 | tf_op jit(solution)/shard_map/ppermute | solution.py:26
  40.1 6.2 %collective-permute-done.5 = bf16[1,180,128]{2,1,0:T(8,128)(2,1)S(1)} collective-permute-done((bf16[1,180,128]{2,1,0:T(8,128)(2,1)S(1)}, bf16[1,180,128]{2,1,0:T(8,128)(2,1)S(1)}, u32[]{:S(2)}, u32[]{:S(2)}) %collective-permute-start.5) | collective-permute-done | bytes 46112 | tf_op jit(solution)/shard_map/ppermute | solution.py:26
  46.3 6.2 %collective-permute-done.6 = bf16[1,180,128]{2,1,0:T(8,128)(2,1)S(1)} collective-permute-done((bf16[1,180,128]{2,1,0:T(8,128)(2,1)S(1)}, bf16[1,180,128]{2,1,0:T(8,128)(2,1)S(1)}, u32[]{:S(2)}, u32[]{:S(2)}) %collective-permute-start.6) | collective-permute-done | bytes 46112 | tf_op jit(solution)/shard_map/ppermute | solution.py:26
  52.5 6.2 %collective-permute-done.7 = bf16[1,180,128]{2,1,0:T(8,128)(2,1)S(1)} collective-permute-done((bf16[1,180,128]{2,1,0:T(8,128)(2,1)S(1)}, bf16[1,180,128]{2,1,0:T(8,128)(2,1)S(1)}, u32[]{:S(2)}, u32[]{:S(2)}) %collective-permute-start.7) | collective-permute-done | bytes 46112 | tf_op jit(solution)/shard_map/ppermute | solution.py:26
  58.7 6.2 %collective-permute-done.8 = bf16[1,180,128]{2,1,0:T(8,128)(2,1)S(1)} collective-permute-done((bf16[1,180,128]{2,1,0:T(8,128)(2,1)S(1)}, bf16[1,180,128]{2,1,0:T(8,128)(2,1)S(1)}, u32[]{:S(2)}, u32[]{:S(2)}) %collective-permute-start.8) | collective-permute-done | bytes 46112 | tf_op jit(solution)/shard_map/ppermute | solution.py:26
  64.9 6.2 %collective-permute-done.9 = bf16[1,180,128]{2,1,0:T(8,128)(2,1)S(1)} collective-permute-done((bf16[1,180,128]{2,1,0:T(8,128)(2,1)S(1)}, bf16[1,180,128]{2,1,0:T(8,128)(2,1)S(1)}, u32[]{:S(2)}, u32[]{:S(2)}) %collective-permute-start.9) | collective-permute-done | bytes 46112 | tf_op jit(solution)/shard_map/ppermute | solution.py:26
  71.1 6.2 %collective-permute-done.10 = bf16[1,180,128]{2,1,0:T(8,128)(2,1)S(1)} collective-permute-done((bf16[1,180,128]{2,1,0:T(8,128)(2,1)S(1)}, bf16[1,180,128]{2,1,0:T(8,128)(2,1)S(1)}, u32[]{:S(2)}, u32[]{:S(2)}) %collective-permute-start.10) | collective-permute-done | bytes 46112 | tf_op jit(solution)/shard_map/ppermute | solution.py:26
  77.2 6.2 %collective-permute-done.11 = bf16[1,180,128]{2,1,0:T(8,128)(2,1)S(1)} collective-permute-done((bf16[1,180,128]{2,1,0:T(8,128)(2,1)S(1)}, bf16[1,180,128]{2,1,0:T(8,128)(2,1)S(1)}, u32[]{:S(2)}, u32[]{:S(2)}) %collective-permute-start.11) | collective-permute-done | bytes 46112 | tf_op jit(solution)/shard_map/ppermute | solution.py:26
  83.4 6.2 %collective-permute-done.12 = bf16[1,180,128]{2,1,0:T(8,128)(2,1)S(1)} collective-permute-done((bf16[1,180,128]{2,1,0:T(8,128)(2,1)S(1)}, bf16[1,180,128]{2,1,0:T(8,128)(2,1)S(1)}, u32[]{:S(2)}, u32[]{:S(2)}) %collective-permute-start.12) | collective-permute-done | bytes 46112 | tf_op jit(solution)/shard_map/ppermute | solution.py:26
  89.6 6.2 %collective-permute-done.13 = bf16[1,180,128]{2,1,0:T(8,128)(2,1)S(1)} collective-permute-done((bf16[1,180,128]{2,1,0:T(8,128)(2,1)S(1)}, bf16[1,180,128]{2,1,0:T(8,128)(2,1)S(1)}, u32[]{:S(2)}, u32[]{:S(2)}) %collective-permute-start.13) | collective-permute-done | bytes 46112 | tf_op jit(solution)/shard_map/ppermute | solution.py:26
  96.3 3.2 %dynamic_update_slice.52 = bf16[16,180,128]{2,0,1:T(8,128)(2,1)S(1)} dynamic-update-slice(bf16[16,180,128]{2,0,1:T(8,128)(2,1)S(1)} %broadcast_in_dim.58, bf16[1,180,128]{2,0,1:T(2,128)(2,1)S(1)} %copy.55, s32[]{:T(128)S(6)} %select_n.170, s32[]{:T(128)} %copy.102, s32[]{:T(128)} %copy.102) | dynamic-update-slice | bytes 92164 | tf_op jit(solution)/shard_map/dynamic_update_slice | solution.py:24
  99.6 3.0 %dynamic_update_slice.53 = bf16[16,180,128]{2,0,1:T(8,128)(2,1)S(1)} dynamic-update-slice(bf16[16,180,128]{2,0,1:T(8,128)(2,1)S(1)} %dynamic_update_slice.52, bf16[1,180,128]{2,0,1:T(2,128)(2,1)S(1)} %copy.56, s32[]{:T(128)S(6)} %select_n.172, s32[]{:T(128)} %copy.102, s32[]{:T(128)} %copy.102) | dynamic-update-slice | bytes 92164 | tf_op jit(solution)/shard_map/dynamic_update_slice | solution.py:24
  102.8 3.0 %dynamic_update_slice.54 = bf16[16,180,128]{2,0,1:T(8,128)(2,1)S(1)} dynamic-update-slice(bf16[16,180,128]{2,0,1:T(8,128)(2,1)S(1)} %dynamic_update_slice.53, bf16[1,180,128]{2,0,1:T(2,128)(2,1)S(1)} %copy.57, s32[]{:T(128)S(6)} %select_n.174, s32[]{:T(128)} %copy.102, s32[]{:T(128)} %copy.102) | dynamic-update-slice | bytes 92164 | tf_op jit(solution)/shard_map/dynamic_update_slice | solution.py:24
  105.9 3.0 %dynamic_update_slice.55 = bf16[16,180,128]{2,0,1:T(8,128)(2,1)S(1)} dynamic-update-slice(bf16[16,180,128]{2,0,1:T(8,128)(2,1)S(1)} %dynamic_update_slice.54, bf16[1,180,128]{2,0,1:T(2,128)(2,1)S(1)} %copy.58, s32[]{:T(128)S(6)} %select_n.176, s32[]{:T(128)} %copy.102, s32[]{:T(128)} %copy.102) | dynamic-update-slice | bytes 92164 | tf_op jit(solution)/shard_map/dynamic_update_slice | solution.py:24
  109.0 3.0 %dynamic_update_slice.56 = bf16[16,180,128]{2,0,1:T(8,128)(2,1)S(1)} dynamic-update-slice(bf16[16,180,128]{2,0,1:T(8,128)(2,1)S(1)} %dynamic_update_slice.55, bf16[1,180,128]{2,0,1:T(2,128)(2,1)S(1)} %copy.59, s32[]{:T(128)S(6)} %select_n.178, s32[]{:T(128)} %copy.102, s32[]{:T(128)} %copy.102) | dynamic-update-slice | bytes 92164 | tf_op jit(solution)/shard_map/dynamic_update_slice | solution.py:24
  112.1 3.0 %dynamic_update_slice.57 = bf16[16,180,128]{2,0,1:T(8,128)(2,1)S(1)} dynamic-update-slice(bf16[16,180,128]{2,0,1:T(8,128)(2,1)S(1)} %dynamic_update_slice.56, bf16[1,180,128]{2,0,1:T(2,128)(2,1)S(1)} %copy.60, s32[]{:T(128)S(6)} %select_n.180, s32[]{:T(128)} %copy.102, s32[]{:T(128)} %copy.102) | dynamic-update-slice | bytes 92164 | tf_op jit(solution)/shard_map/dynamic_update_slice | solution.py:24
  115.3 3.0 %dynamic_update_slice.58 = bf16[16,180,128]{2,0,1:T(8,128)(2,1)S(1)} dynamic-update-slice(bf16[16,180,128]{2,0,1:T(8,128)(2,1)S(1)} %dynamic_update_slice.57, bf16[1,180,128]{2,0,1:T(2,128)(2,1)S(1)} %copy.61, s32[]{:T(128)S(6)} %select_n.182, s32[]{:T(128)} %copy.102, s32[]{:T(128)} %copy.102) | dynamic-update-slice | bytes 92164 | tf_op jit(solution)/shard_map/dynamic_update_slice | solution.py:24
  118.4 3.0 %dynamic_update_slice.59 = bf16[16,180,128]{2,0,1:T(8,128)(2,1)S(1)} dynamic-update-slice(bf16[16,180,128]{2,0,1:T(8,128)(2,1)S(1)} %dynamic_update_slice.58, bf16[1,180,128]{2,0,1:T(2,128)(2,1)S(1)} %copy.62, s32[]{:T(128)S(6)} %select_n.184, s32[]{:T(128)} %copy.102, s32[]{:T(128)} %copy.102) | dynamic-update-slice | bytes 92164 | tf_op jit(solution)/shard_map/dynamic_update_slice | solution.py:24
  121.5 3.0 %dynamic_update_slice.60 = bf16[16,180,128]{2,0,1:T(8,128)(2,1)S(1)} dynamic-update-slice(bf16[16,180,128]{2,0,1:T(8,128)(2,1)S(1)} %dynamic_update_slice.59, bf16[1,180,128]{2,0,1:T(2,128)(2,1)S(1)} %copy.63, s32[]{:T(128)S(6)} %select_n.186, s32[]{:T(128)} %copy.102, s32[]{:T(128)} %copy.102) | dynamic-update-slice | bytes 92164 | tf_op jit(solution)/shard_map/dynamic_update_slice | solution.py:24
  124.7 3.0 %dynamic_update_slice.61 = bf16[16,180,128]{2,0,1:T(8,128)(2,1)S(1)} dynamic-update-slice(bf16[16,180,128]{2,0,1:T(8,128)(2,1)S(1)} %dynamic_update_slice.60, bf16[1,180,128]{2,0,1:T(2,128)(2,1)S(1)} %copy.64, s32[]{:T(128)S(6)} %select_n.188, s32[]{:T(128)} %copy.102, s32[]{:T(128)} %copy.102) | dynamic-update-slice | bytes 92164 | tf_op jit(solution)/shard_map/dynamic_update_slice | solution.py:24
  127.8 3.0 %dynamic_update_slice.62 = bf16[16,180,128]{2,0,1:T(8,128)(2,1)S(1)} dynamic-update-slice(bf16[16,180,128]{2,0,1:T(8,128)(2,1)S(1)} %dynamic_update_slice.61, bf16[1,180,128]{2,0,1:T(2,128)(2,1)S(1)} %copy.65, s32[]{:T(128)S(6)} %select_n.190, s32[]{:T(128)} %copy.102, s32[]{:T(128)} %copy.102) | dynamic-update-slice | bytes 92164 | tf_op jit(solution)/shard_map/dynamic_update_slice | solution.py:24
  131.0 3.0 %dynamic_update_slice.63 = bf16[16,180,128]{2,0,1:T(8,128)(2,1)S(1)} dynamic-update-slice(bf16[16,180,128]{2,0,1:T(8,128)(2,1)S(1)} %dynamic_update_slice.62, bf16[1,180,128]{2,0,1:T(2,128)(2,1)S(1)} %copy.66, s32[]{:T(128)S(6)} %select_n.192, s32[]{:T(128)} %copy.102, s32[]{:T(128)} %copy.102) | dynamic-update-slice | bytes 92164 | tf_op jit(solution)/shard_map/dynamic_update_slice | solution.py:24
  134.1 3.0 %dynamic_update_slice.64 = bf16[16,180,128]{2,0,1:T(8,128)(2,1)S(1)} dynamic-update-slice(bf16[16,180,128]{2,0,1:T(8,128)(2,1)S(1)} %dynamic_update_slice.63, bf16[1,180,128]{2,0,1:T(2,128)(2,1)S(1)} %copy.67, s32[]{:T(128)S(6)} %select_n.194, s32[]{:T(128)} %copy.102, s32[]{:T(128)} %copy.102) | dynamic-update-slice | bytes 92164 | tf_op jit(solution)/shard_map/dynamic_update_slice | solution.py:24
  137.2 3.0 %dynamic_update_slice.65 = bf16[16,180,128]{2,0,1:T(8,128)(2,1)S(1)} dynamic-update-slice(bf16[16,180,128]{2,0,1:T(8,128)(2,1)S(1)} %dynamic_update_slice.64, bf16[1,180,128]{2,0,1:T(2,128)(2,1)S(1)} %copy.68, s32[]{:T(128)S(6)} %select_n.196, s32[]{:T(128)} %copy.102, s32[]{:T(128)} %copy.102) | dynamic-update-slice | bytes 92164 | tf_op jit(solution)/shard_map/dynamic_update_slice | solution.py:24
  140.4 3.0 %dynamic_update_slice.66 = bf16[16,180,128]{2,0,1:T(8,128)(2,1)S(1)} dynamic-update-slice(bf16[16,180,128]{2,0,1:T(8,128)(2,1)S(1)} %dynamic_update_slice.65, bf16[1,180,128]{2,0,1:T(2,128)(2,1)S(1)} %copy.69, s32[]{:T(128)S(6)} %select_n.198, s32[]{:T(128)} %copy.102, s32[]{:T(128)} %copy.102) | dynamic-update-slice | bytes 92164 | tf_op jit(solution)/shard_map/dynamic_update_slice | solution.py:24
  143.5 3.0 %dynamic_update_slice.67 = bf16[16,180,128]{2,0,1:T(8,128)(2,1)S(1)} dynamic-update-slice(bf16[16,180,128]{2,0,1:T(8,128)(2,1)S(1)} %dynamic_update_slice.66, bf16[1,180,128]{2,0,1:T(2,128)(2,1)S(1)} %copy.70, s32[]{:T(128)S(6)} %select_n.200, s32[]{:T(128)} %copy.102, s32[]{:T(128)} %copy.102) | dynamic-update-slice | bytes 92164 | tf_op jit(solution)/shard_map/dynamic_update_slice | solution.py:24
  146.6 0.9 copy-done.1
  147.6 18.0 %all-gather = bf16[16,1,180]{2,1,0:T(2,128)(2,1)S(1)} all-gather(bf16[1,1,180]{2,1,0:T(2,128)(2,1)S(1)} %fusion.13), channel_id=1, replica_groups=mesh['query'=2,'gallery'=16] {'gallery'}, dimensions={0}, use_global_device_ids=true | all-gather | bytes 6120 | tf_op jit(solution)/shard_map/all_gather | solution.py:56
  165.6 4.7 %all-gather.1 = bf16[2,180,16]{1,2,0:T(8,128)(2,1)S(1)} all-gather(bf16[1,180,16]{1,2,0:T(8,128)(2,1)S(1)} %bitcast.56), channel_id=1, replica_groups=mesh['query'=2,'gallery'=16] {'query'}, dimensions={0}, use_global_device_ids=true | all-gather | bytes 17280 | tf_op jit(solution)/shard_map/all_gather | solution.py:60
  170.6 0.6 multiply_reduce_fusion.1
  171.4 4.1 %all-gather.4.cloned.1.call-done = bf16[16,360,128]{2,0,1:T(8,128)(2,1)} async-done(((bf16[16,180,128]{2,0,1:T(8,128)(2,1)}), bf16[16,360,128]{2,0,1:T(8,128)(2,1)}) %all-gather.4.cloned.1.call-update) | async-done | bytes 1474576 | tf_op jit(solution)/shard_map/all_gather | solution.py:59
  175.5 1.8 copy.71
  177.2 9.6 %while.12 = (s32[]{:T(128)}, f32[4,768,4,2]{1,3,2,0:T(2,128)S(1)}, bf16[4,1,1440]{2,1,0:T(2,128)(2,1)S(1)}, bf16[4,1440,128]{2,1,0:T(8,128)(2,1)S(1)}, bf16[768,128]{1,0:T(8,128)(2,1)S(1)}, /*index=5*/s32[]{:T(128)}) while((s32[]{:T(128)}, f32[4,768,4,2]{1,3,2,0:T(2,128)S(1)}, bf16[4,1,1440]{2,1,0:T(2,128)(2,1)S(1)}, ...), condition=%wide.region_6.7_spmd.clone.clone, body=%wide.region_3.6_spmd.clone.clone.sunk | while | flops 288650176 | bytes 9543377 | solution.py:79
  177.3 1.1 convolution_select_fusion.2
  178.4 1.1 select_reduce_fusion.3
  179.7 1.1 convolution_select_fusion.2
  180.8 1.1 select_reduce_fusion.3
  182.1 1.1 convolution_select_fusion.2
  183.2 1.1 select_reduce_fusion.3
  184.5 1.1 convolution_select_fusion.2
  185.6 1.1 select_reduce_fusion.3
  187.2 0.7 copy.74
  (82 shorter events, 2.9 us)
Async XLA Ops:
  6.5 164.0 %copy-start = (bf16[24,32,768]{2,1,0:T(8,128)(2,1)S(1)}, bf16[24,32,768]{2,1,0:T(8,128)(2,1)}, u32[]{:S(2)}) copy-start(bf16[24,32,768]{2,1,0:T(8,128)(2,1)} %param.8) | copy-start | bytes 3538948
  6.5 168.9 %all-gather.4.cloned.1.call-start = ((), (), s32[]{:S(2)}) async-start(), calls=%async_computation | async-start | bytes 2211840 | tf_op jit(solution)/shard_map/all_gather | solution.py:59
  8.1 7.3 %collective-permute-start = (bf16[1,180,128]{2,1,0:T(8,128)(2,1)S(1)}, bf16[1,180,128]{2,1,0:T(8,128)(2,1)S(1)}, u32[]{:S(2)}, u32[]{:S(2)}) collective-permute-start(bf16[1,180,128]{2,1,0:T(8,128)(2,1)S(1)} %fusion.11), channel_id=1, source_target_pairs={{0,1},{1,2},{2,3},{3,4},{4,5},{5,6},{6,7},{7,8},{8,9},{9,10},{10,1... | collective-permute-start | bytes 138248 | tf_op jit(solution)/shard_map/ppermute | solution.py:26
  15.3 6.2 %collective-permute-start.1 = (bf16[1,180,128]{2,1,0:T(8,128)(2,1)S(1)}, bf16[1,180,128]{2,1,0:T(8,128)(2,1)S(1)}, u32[]{:S(2)}, u32[]{:S(2)}) collective-permute-start(bf16[1,180,128]{2,1,0:T(8,128)(2,1)S(1)} %collective-permute-done), channel_id=1, source_target_pairs={{0,1},{1,2},{2,3},{3,4},{4,5},{5,6},{6,7},{7,8},{8,9},{9,10},{10,1... | collective-permute-start | bytes 138248 | tf_op jit(solution)/shard_map/ppermute | solution.py:26
  21.5 6.2 %collective-permute-start.2 = (bf16[1,180,128]{2,1,0:T(8,128)(2,1)S(1)}, bf16[1,180,128]{2,1,0:T(8,128)(2,1)S(1)}, u32[]{:S(2)}, u32[]{:S(2)}) collective-permute-start(bf16[1,180,128]{2,1,0:T(8,128)(2,1)S(1)} %collective-permute-done.1), channel_id=1, source_target_pairs={{0,1},{1,2},{2,3},{3,4},{4,5},{5,6},{6,7},{7,8},{8,9},{9,10},{10,1... | collective-permute-start | bytes 138248 | tf_op jit(solution)/shard_map/ppermute | solution.py:26
  27.7 6.2 %collective-permute-start.3 = (bf16[1,180,128]{2,1,0:T(8,128)(2,1)S(1)}, bf16[1,180,128]{2,1,0:T(8,128)(2,1)S(1)}, u32[]{:S(2)}, u32[]{:S(2)}) collective-permute-start(bf16[1,180,128]{2,1,0:T(8,128)(2,1)S(1)} %collective-permute-done.2), channel_id=1, source_target_pairs={{0,1},{1,2},{2,3},{3,4},{4,5},{5,6},{6,7},{7,8},{8,9},{9,10},{10,1... | collective-permute-start | bytes 138248 | tf_op jit(solution)/shard_map/ppermute | solution.py:26
  33.9 6.2 %collective-permute-start.4 = (bf16[1,180,128]{2,1,0:T(8,128)(2,1)S(1)}, bf16[1,180,128]{2,1,0:T(8,128)(2,1)S(1)}, u32[]{:S(2)}, u32[]{:S(2)}) collective-permute-start(bf16[1,180,128]{2,1,0:T(8,128)(2,1)S(1)} %collective-permute-done.3), channel_id=1, source_target_pairs={{0,1},{1,2},{2,3},{3,4},{4,5},{5,6},{6,7},{7,8},{8,9},{9,10},{10,1... | collective-permute-start | bytes 138248 | tf_op jit(solution)/shard_map/ppermute | solution.py:26
  40.1 6.2 %collective-permute-start.5 = (bf16[1,180,128]{2,1,0:T(8,128)(2,1)S(1)}, bf16[1,180,128]{2,1,0:T(8,128)(2,1)S(1)}, u32[]{:S(2)}, u32[]{:S(2)}) collective-permute-start(bf16[1,180,128]{2,1,0:T(8,128)(2,1)S(1)} %collective-permute-done.4), channel_id=1, source_target_pairs={{0,1},{1,2},{2,3},{3,4},{4,5},{5,6},{6,7},{7,8},{8,9},{9,10},{10,1... | collective-permute-start | bytes 138248 | tf_op jit(solution)/shard_map/ppermute | solution.py:26
  46.3 6.2 %collective-permute-start.6 = (bf16[1,180,128]{2,1,0:T(8,128)(2,1)S(1)}, bf16[1,180,128]{2,1,0:T(8,128)(2,1)S(1)}, u32[]{:S(2)}, u32[]{:S(2)}) collective-permute-start(bf16[1,180,128]{2,1,0:T(8,128)(2,1)S(1)} %collective-permute-done.5), channel_id=1, source_target_pairs={{0,1},{1,2},{2,3},{3,4},{4,5},{5,6},{6,7},{7,8},{8,9},{9,10},{10,1... | collective-permute-start | bytes 138248 | tf_op jit(solution)/shard_map/ppermute | solution.py:26
  52.5 6.2 %collective-permute-start.7 = (bf16[1,180,128]{2,1,0:T(8,128)(2,1)S(1)}, bf16[1,180,128]{2,1,0:T(8,128)(2,1)S(1)}, u32[]{:S(2)}, u32[]{:S(2)}) collective-permute-start(bf16[1,180,128]{2,1,0:T(8,128)(2,1)S(1)} %collective-permute-done.6), channel_id=1, source_target_pairs={{0,1},{1,2},{2,3},{3,4},{4,5},{5,6},{6,7},{7,8},{8,9},{9,10},{10,1... | collective-permute-start | bytes 138248 | tf_op jit(solution)/shard_map/ppermute | solution.py:26
  58.7 6.2 %collective-permute-start.8 = (bf16[1,180,128]{2,1,0:T(8,128)(2,1)S(1)}, bf16[1,180,128]{2,1,0:T(8,128)(2,1)S(1)}, u32[]{:S(2)}, u32[]{:S(2)}) collective-permute-start(bf16[1,180,128]{2,1,0:T(8,128)(2,1)S(1)} %collective-permute-done.7), channel_id=1, source_target_pairs={{0,1},{1,2},{2,3},{3,4},{4,5},{5,6},{6,7},{7,8},{8,9},{9,10},{10,1... | collective-permute-start | bytes 138248 | tf_op jit(solution)/shard_map/ppermute | solution.py:26
  64.9 6.2 %collective-permute-start.9 = (bf16[1,180,128]{2,1,0:T(8,128)(2,1)S(1)}, bf16[1,180,128]{2,1,0:T(8,128)(2,1)S(1)}, u32[]{:S(2)}, u32[]{:S(2)}) collective-permute-start(bf16[1,180,128]{2,1,0:T(8,128)(2,1)S(1)} %collective-permute-done.8), channel_id=1, source_target_pairs={{0,1},{1,2},{2,3},{3,4},{4,5},{5,6},{6,7},{7,8},{8,9},{9,10},{10,1... | collective-permute-start | bytes 138248 | tf_op jit(solution)/shard_map/ppermute | solution.py:26
  71.1 6.2 %collective-permute-start.10 = (bf16[1,180,128]{2,1,0:T(8,128)(2,1)S(1)}, bf16[1,180,128]{2,1,0:T(8,128)(2,1)S(1)}, u32[]{:S(2)}, u32[]{:S(2)}) collective-permute-start(bf16[1,180,128]{2,1,0:T(8,128)(2,1)S(1)} %collective-permute-done.9), channel_id=1, source_target_pairs={{0,1},{1,2},{2,3},{3,4},{4,5},{5,6},{6,7},{7,8},{8,9},{9,10},{10,1... | collective-permute-start | bytes 138248 | tf_op jit(solution)/shard_map/ppermute | solution.py:26
  77.2 6.2 %collective-permute-start.11 = (bf16[1,180,128]{2,1,0:T(8,128)(2,1)S(1)}, bf16[1,180,128]{2,1,0:T(8,128)(2,1)S(1)}, u32[]{:S(2)}, u32[]{:S(2)}) collective-permute-start(bf16[1,180,128]{2,1,0:T(8,128)(2,1)S(1)} %collective-permute-done.10), channel_id=1, source_target_pairs={{0,1},{1,2},{2,3},{3,4},{4,5},{5,6},{6,7},{7,8},{8,9},{9,10},{10,1... | collective-permute-start | bytes 138248 | tf_op jit(solution)/shard_map/ppermute | solution.py:26
  83.4 6.2 %collective-permute-start.12 = (bf16[1,180,128]{2,1,0:T(8,128)(2,1)S(1)}, bf16[1,180,128]{2,1,0:T(8,128)(2,1)S(1)}, u32[]{:S(2)}, u32[]{:S(2)}) collective-permute-start(bf16[1,180,128]{2,1,0:T(8,128)(2,1)S(1)} %collective-permute-done.11), channel_id=1, source_target_pairs={{0,1},{1,2},{2,3},{3,4},{4,5},{5,6},{6,7},{7,8},{8,9},{9,10},{10,1... | collective-permute-start | bytes 138248 | tf_op jit(solution)/shard_map/ppermute | solution.py:26
  89.6 6.2 %collective-permute-start.13 = (bf16[1,180,128]{2,1,0:T(8,128)(2,1)S(1)}, bf16[1,180,128]{2,1,0:T(8,128)(2,1)S(1)}, u32[]{:S(2)}, u32[]{:S(2)}) collective-permute-start(bf16[1,180,128]{2,1,0:T(8,128)(2,1)S(1)} %collective-permute-done.12), channel_id=1, source_target_pairs={{0,1},{1,2},{2,3},{3,4},{4,5},{5,6},{6,7},{7,8},{8,9},{9,10},{10,1... | collective-permute-start | bytes 138248 | tf_op jit(solution)/shard_map/ppermute | solution.py:26
  95.8 47.6 %collective-permute-start.14 = (bf16[1,180,128]{2,1,0:T(8,128)(2,1)S(1)}, bf16[1,180,128]{2,1,0:T(8,128)(2,1)S(1)}, u32[]{:S(2)}, u32[]{:S(2)}) collective-permute-start(bf16[1,180,128]{2,1,0:T(8,128)(2,1)S(1)} %collective-permute-done.13), channel_id=1, source_target_pairs={{0,1},{1,2},{2,3},{3,4},{4,5},{5,6},{6,7},{7,8},{8,9},{9,10},{10,1... | collective-permute-start | bytes 138248 | tf_op jit(solution)/shard_map/ppermute | solution.py:26
  124.7 22.8 %copy-start.5 = (s32[2]{0:T(128)S(1)}, s32[2]{0:T(128)}, u32[]{:S(2)}) copy-start(s32[2]{0:T(128)} %param.12) | copy-start | bytes 28
  124.7 22.9 %copy-start.4 = (s32[1,180]{1,0:T(1,128)S(1)}, s32[1,180]{1,0:T(1,128)}, u32[]{:S(2)}) copy-start(s32[1,180]{1,0:T(1,128)} %param.11) | copy-start | bytes 2164
  127.7 42.8 %copy-start.2 = (bf16[768,128]{1,0:T(8,128)(2,1)S(1)}, bf16[768,128]{1,0:T(8,128)(2,1)}, u32[]{:S(2)}) copy-start(bf16[768,128]{1,0:T(8,128)(2,1)} %param.13) | copy-start | bytes 589828
  146.5 0.9 copy-start.1
  147.6 23.8 %copy-start.3 = (s32[24,32]{1,0:T(8,128)S(1)}, s32[24,32]{1,0:T(8,128)}, u32[]{:S(2)}) copy-start(s32[24,32]{1,0:T(8,128)} %param.9) | copy-start | bytes 9220
Sparse Core Ops, SparseCore 0:
  147.6 27.8 all-gather.3
